TPU v7x, 32 devices: a whole 2x2x4 slice. The times are simulated.
32 devices in a mesh: chan: 8 (over z, y), tm: 4 (over x, core).
Axes of the slice: x: 2, y: 2, z: 4, core: 2. Of those that a mesh axis runs over, the one named last changes fastest.
Arguments:
- strain_rate: float32 [2048, 4096], P('tm', 'chan'), may hold values from -6 to 6
- gauge: float32 [4096], P('chan'), may hold values from 0.02 to 0.2
- valid: int32 [4096], P('chan'), may hold values 0 or 1
- segment: int32 [4096], P('chan'), may hold values from 0 to 3, never falling along the last dimension, each value on 1 to 2048 neighbouring positions
- stencil: float32 [3, 4096], P(None, 'chan'), may hold values from 0.1 to 0.6
Outputs:
- strain_out: float32 [2048, 4096], P('tm', 'chan')
- velocity: float32 [2048, 4096], P('tm', 'chan')
Inputs may be any that keep to these rules, and one draw needn't show every extreme that they name: Ids never fall along the fiber; each segment covers 1 to 2048 neighbouring channels, one exactly 2048.
All inputs are finite; a program needn't handle non-finite values. No bound on the sum of `valid` on one device may be relied on, other than what follows from the above.
Results may differ from a plain program's by a relative error of at most 0.0003.
Values sent between devices are 32-bit elements; how exact they have to be, the bound alone decides.
A program may use at most 64 MiB of HBM per device.

v0:
```python
import jax
import jax.numpy as jnp
from jax import lax
from jax.sharding import PartitionSpec as P

precise = lax.Precision.HIGHEST


def prefix_2(part, axis, combine, identity):
    place = lax.axis_index(axis)
    gathered = jax.tree.map(lambda a: lax.all_gather(a, axis), part)
    state = jax.tree.map(lambda a, e: jnp.zeros_like(a) + jnp.asarray(e, a.dtype), part, identity)

    def one(hop, state):
        return combine(
            state, jax.tree.map(lambda a: lax.dynamic_index_in_dim(a, hop, 0, False), gathered)
        )

    return lax.fori_loop(0, place, one, state)


def padded_2(block, sides, width):
    for axis, dim in sides:
        count = lax.axis_size(axis)
        forward = [(i, i + 1) for i in range(count - 1)]
        backward = [(target, source) for source, target in forward]
        low = lax.ppermute(
            lax.slice_in_dim(block, block.shape[dim] - width, None, axis=dim), axis, forward
        )
        high = lax.ppermute(lax.slice_in_dim(block, 0, width, axis=dim), axis, backward)
        block = jnp.concatenate([low, block, high], axis=dim)
    return block


def compose(early, later):
    return (
        jnp.dot(later[0], early[0], precision=precise),
        jnp.dot(later[0], early[1], precision=precise) + later[1],
    )


def join_blocks(early, later):
    early_sum, early_head, early_tail = early
    later_sum, later_head, later_tail = later
    later_empty = later_head < 0.0
    early_empty = early_head < 0.0
    same = (later_head == later_tail) & (later_head == early_tail)
    total = jnp.where(later_empty, early_sum, jnp.where(same, early_sum + later_sum, later_sum))
    head = jnp.where(early_empty, later_head, early_head)
    tail = jnp.where(later_empty, early_tail, later_tail)
    return (total, head, tail)


def segment_matrix(idents):
    width = idents.shape[0]
    position = jnp.arange(width)
    upper = position[:, None] <= position[None, :]
    return jnp.where(upper & (idents[:, None] == idents[None, :]), 1.0, 0.0).astype(jnp.float32)


def on_device(strain_rate, gauge, valid, segment, stencil):
    slab, chans = strain_rate.shape
    pole_one = 1.0 - 1.0 / (2.0 * slab)
    pole_two = 1.0 - 1.0 / (8.0 * slab)
    integ_gain = 1.0 / (8.0 * slab) ** 0.5
    sample_pos = jnp.arange(slab, dtype=jnp.float32)
    offset = sample_pos[:, None] - sample_pos[None, :]
    lower = offset >= 0.0
    safe = jnp.maximum(offset, 0.0)
    smooth_one = jnp.where(lower, (1.0 - pole_one) * pole_one**safe, 0.0)
    smooth_two = jnp.where(lower, (1.0 - pole_two) * pole_two**safe, 0.0)
    summing = jnp.where(lower, 1.0, 0.0).astype(jnp.float32)
    decay_one = pole_one ** (sample_pos + 1.0)
    decay_two = pole_two ** (sample_pos + 1.0)
    passone = strain_rate - jnp.dot(smooth_one, strain_rate, precision=precise)
    passtwo = passone - jnp.dot(smooth_two, passone, precision=precise)
    strain_zero = integ_gain * jnp.dot(summing, passtwo, precision=precise)
    ends = jnp.stack([strain_rate[-1] - passone[-1], passone[-1] - passtwo[-1], strain_zero[-1]])
    resp_one = decay_one - jnp.dot(smooth_two, decay_one, precision=precise)
    cum_one = integ_gain * jnp.dot(summing, resp_one, precision=precise)
    cum_two = integ_gain * jnp.dot(summing, decay_two, precision=precise)
    nought = jnp.zeros((), jnp.float32)
    unity = jnp.ones((), jnp.float32)
    transfer = jnp.stack(
        [
            jnp.stack([decay_one[-1], nought, nought]),
            jnp.stack([resp_one[-1] - decay_one[-1], decay_two[-1], nought]),
            jnp.stack([-cum_one[-1], -cum_two[-1], unity]),
        ]
    )
    prefix = prefix_2(
        (transfer, ends), "tm", compose, (jnp.eye(3, dtype=jnp.float32), jnp.zeros_like(ends))
    )
    incoming = prefix[1]
    filtered = (
        passtwo
        - resp_one[:, None] * incoming[0][None, :]
        - decay_two[:, None] * incoming[1][None, :]
    )
    strain_out = (
        strain_zero
        - cum_one[:, None] * incoming[0][None, :]
        - cum_two[:, None] * incoming[1][None, :]
        + incoming[2][None, :]
    )
    scaled = filtered * (gauge * valid.astype(jnp.float32))[None, :]
    local = jnp.dot(scaled, segment_matrix(segment), precision=precise)
    idents_float = segment.astype(jnp.float32)
    element = (local[:, -1], idents_float[:1], idents_float[-1:])
    empty = (
        jnp.zeros((slab,), jnp.float32),
        -jnp.ones((1,), jnp.float32),
        -jnp.ones((1,), jnp.float32),
    )
    carried, head_in, tail_in = prefix_2(element, "chan", join_blocks, empty)
    integrated = local + jnp.where(idents_float == tail_in, 1.0, 0.0)[None, :] * carried[:, None]
    padded = padded_2(integrated, (("chan", 1),), 1)
    velocity = (
        stencil[0][None, :] * padded[:, :-2]
        + stencil[1][None, :] * padded[:, 1:-1]
        + stencil[2][None, :] * padded[:, 2:]
    )
    return (strain_out, velocity)


def solution(mesh):
    in_specs = (P("tm", "chan"), P("chan"), P("chan"), P("chan"), P(None, "chan"))
    out_specs = (P("tm", "chan"), P("tm", "chan"))
    return jax.shard_map(
        on_device, mesh=mesh, in_specs=in_specs, out_specs=out_specs, check_vma=False
    )
```

profile of v0, /device:TPU:26, one launch (start us, length us, event | category | flops | bytes accessed | tf_op | source)
XLA Modules:
  0.0 117.8 jit_solution(8858140758040933968)
XLA Ops:
  0.7 3.8 %convolution_subtract_fusion.1 = f32[512,512]{1,0:T(8,128)S(1)} fusion(f32[512,512]{1,0:T(8,128)} %param.9), kind=kOutput, calls=%fused_computation.16 | convolution fusion | flops 1612185600 | bytes 2097152 | tf_op jit(solution)/shard_map/dot_general | solution.py:75
  4.5 2.2 %convolution_subtract_fusion = f32[512,512]{1,0:T(8,128)S(1)} fusion(f32[512,512]{1,0:T(8,128)S(1)} %convolution_subtract_fusion.1), kind=kOutput, calls=%fused_computation.15 | convolution fusion | flops 1612185600 | bytes 2097152 | tf_op jit(solution)/shard_map/dot_general | solution.py:76
  6.7 0.7 slice_subtract_fusion.1
  7.4 2.0 %fusion.10 = f32[512,512]{1,0:T(8,128)S(1)} fusion(f32[512,512]{1,0:T(8,128)S(1)} %convolution_subtract_fusion), kind=kOutput, calls=%fused_computation.17 | convolution fusion | flops 1611661312 | bytes 2097152 | tf_op jit(solution)/shard_map/dot_general | solution.py:77
  10.1 1.3 %fusion.34 = f32[1,512]{1,0:T(1,128)S(1)} fusion(f32[512,1]{0,1:T(1,128)S(1)} %bitcast.73), kind=kOutput, calls=%fused_computation.41 | convolution fusion | flops 4456448 | bytes 4096 | tf_op jit(solution)/shard_map/dot_general | solution.py:79
  13.9 1.2 fusion.6
  16.9 1.2 fusion.4
  19.4 0.7 maximum_bitcast_fusion.2
  20.1 5.2 %all-gather.5 = f32[4,3,3]{2,1,0:T(4,128)S(1)} all-gather(f32[1,3,3]{2,1,0:T(4,128)S(1)} %maximum_bitcast_fusion.1), channel_id=2, replica_groups=mesh['chan'=8,'tm'=4] {'tm'}, dimensions={0}, use_global_device_ids=true | all-gather | bytes 180 | tf_op jit(solution)/shard_map/all_gather | solution.py:11
  25.3 5.2 %all-gather.6 = f32[4,3,512]{2,1,0:T(4,128)S(1)} all-gather(f32[1,3,512]{2,1,0:T(4,128)S(1)} %maximum_bitcast_fusion), channel_id=3, replica_groups=mesh['chan'=8,'tm'=4] {'tm'}, dimensions={0}, use_global_device_ids=true | all-gather | bytes 30720 | tf_op jit(solution)/shard_map/all_gather | solution.py:11
  30.8 0.7 copy-done
  31.5 0.7 copy-done.2
  32.2 2.2 %fusion.17 = f32[512,512]{0,1:T(8,128)S(1)} fusion(f32[512,512]{1,0:T(8,128)S(1)} %convolution_subtract_fusion, s32[512]{0:T(512)S(1)} %copy-done, f32[512]{0:T(512)S(1)} %convert_multiply_fusion, f32[512]{0:T(512)S(1)} %fusion.62, f32[512]{0:T(512)S(1)} %fusion.64, f32[512]{0:T(512)S(1)} %bitcast.66, f32[512]{0:T(512)S(1)} %bitcast.63), kind=kOutput, calls=%fused_computation.25 | convolution fusion | flops 1612972032 | bytes 2109440 | tf_op jit(solution)/shard_map/dot_general | solution.py:107
  34.5 22.3 %all-gather.4 = f32[4096,1]{0,1:T(1,128)S(1)} all-gather(f32[512,1]{0,1:T(1,128)S(1)} %slice.99), channel_id=6, replica_groups=mesh['chan'=8,'tm'=4] {'chan'}, dimensions={0}, use_global_device_ids=true | all-gather | bytes 18432 | tf_op jit(solution)/shard_map/all_gather | solution.py:11
  57.3 0.7 reduce.3
  59.3 0.8 slice_dynamic-update-slice_fusion
  60.1 0.7 slice_dynamic-update-slice_fusion.1
  60.8 19.0 %all-reduce.3 = (f32[8]{0:T(128)S(1)}, f32[8]{0:T(128)S(1)}) all-reduce(f32[8]{0:T(128)S(1)} %slice_dynamic-update-slice_fusion.1, f32[8]{0:T(128)S(1)} %slice_dynamic-update-slice_fusion), channel_id=4, replica_groups=mesh['chan'=8,'tm'=4] {'chan'}, use_global_device_ids=true, to_apply=%add.1 | all-reduce | flops 16 | bytes 128
  79.9 23.2 %while.27 = (s32[]{:T(128)}, f32[512]{0:T(512)S(1)}, f32[1]{0:T(128)}, s32[]{:T(128)}, f32[8,1]{0,1:T(1,128)S(1)}, /*index=5*/f32[8,1]{0,1:T(1,128)S(1)}, f32[8,...) while((s32[]{:T(128)}, f32[512]{0:T(512)S(1)}, f32[1]{0:T(128)}, s32[]{:T(128)}, ...), condition=%wide.region_3.4_spmd, body=%wide.region_2.3_spmd.sunk | while | flops 1546 | bytes 10452 | solution.py:19
  103.3 7.3 %collective-permute-start = (f32[512,1]{0,1:T(1,128)S(1)}, f32[512,1]{0,1:T(1,128)S(1)}, u32[]{:S(2)}, u32[]{:S(2)}) collective-permute-start(f32[512,1]{0,1:T(1,128)S(1)} %get-tuple-element.140), channel_id=1, source_target_pairs={{0,4},{4,8},{8,12},{12,16},{16,20},{20,24},{24,28},{1,5},{5,9},{9,... | collective-permute-start | bytes 6152 | tf_op jit(solution)/shard_map/ppermute | solution.py:27
  110.6 1.9 %collective-permute-start.1 = (f32[512,1]{0,1:T(1,128)S(1)}, f32[512,1]{0,1:T(1,128)S(1)}, u32[]{:S(2)}, u32[]{:S(2)}) collective-permute-start(f32[512,1]{0,1:T(1,128)S(1)} %get-tuple-element.141), channel_id=1, source_target_pairs={{4,0},{8,4},{12,8},{16,12},{20,16},{24,20},{28,24},{5,1},{9,5},{13... | collective-permute-start | bytes 6152 | tf_op jit(solution)/shard_map/ppermute | solution.py:30
  112.6 1.2 %subtract_add_fusion = f32[512,512]{1,0:T(8,128)} fusion(f32[512,512]{1,0:T(8,128)S(1)} %fusion.10, f32[512]{0:T(512)S(1)} %bitcast.65, f32[512]{0:T(512)S(1)} %bitcast.67, f32[512]{0:T(512)S(1)} %broadcast_multiply_fusion, f32[512]{0:T(512)S(1)} %bitcast.64, f32[512]{0:T(512)S(1)} %broadcast_multiply_fusion.1), kind=kLoop, calls=%fused_computation.33 | loop fusion | flops 1310720 | bytes 2107392 | tf_op jit(solution)/shard_map/add | solution.py:101
  113.8 2.3 %collective-permute-done.1 = f32[512,1]{0,1:T(1,128)S(1)} collective-permute-done((f32[512,1]{0,1:T(1,128)S(1)}, f32[512,1]{0,1:T(1,128)S(1)}, u32[]{:S(2)}, u32[]{:S(2)}) %collective-permute-start.1) | collective-permute-done | bytes 2080 | tf_op jit(solution)/shard_map/ppermute | solution.py:30
  116.5 1.3 %copy.8 = f32[512,512]{1,0:T(8,128)} copy(f32[512,512]{0,1:T(8,128)S(1)} %fusion.14) | data formatting | bytes 2097152
  (62 shorter events, 10.8 us)
Async XLA Ops:
  30.8 0.7 copy-start
  31.5 0.7 copy-start.2
  31.5 0.7 copy-start.3
  58.0 0.7 copy-start.4
  103.3 10.5 %collective-permute-start = (f32[512,1]{0,1:T(1,128)S(1)}, f32[512,1]{0,1:T(1,128)S(1)}, u32[]{:S(2)}, u32[]{:S(2)}) collective-permute-start(f32[512,1]{0,1:T(1,128)S(1)} %get-tuple-element.140), channel_id=1, source_target_pairs={{0,4},{4,8},{8,12},{12,16},{16,20},{20,24},{24,28},{1,5},{5,9},{9,... | collective-permute-start | bytes 6152 | tf_op jit(solution)/shard_map/ppermute | solution.py:27
  110.6 5.5 %collective-permute-start.1 = (f32[512,1]{0,1:T(1,128)S(1)}, f32[512,1]{0,1:T(1,128)S(1)}, u32[]{:S(2)}, u32[]{:S(2)}) collective-permute-start(f32[512,1]{0,1:T(1,128)S(1)} %get-tuple-element.141), channel_id=1, source_target_pairs={{4,0},{8,4},{12,8},{16,12},{20,16},{24,20},{28,24},{5,1},{9,5},{13... | collective-permute-start | bytes 6152 | tf_op jit(solution)/shard_map/ppermute | solution.py:30
  112.5 1.3 %copy-start.1 = (f32[3,512]{1,0:T(4,128)S(1)}, f32[3,512]{1,0:T(4,128)}, u32[]{:S(2)}) copy-start(f32[3,512]{1,0:T(4,128)} %param.13) | copy-start | bytes 18436
where the time goes:
time: 119 us; the launch traced here: 118 us
  blocking collectives  51.7 us (43%)
  loops' own time  19.2 us (16%)
  matrix products  14.2 us (12%)
  local copies, waits for them, and re-layouts  13.7 us (12%)
  starting transfers between devices  9.24 us (8%)
  other arithmetic  4.12 us (3%)
  between operations  3.38 us (3%)
  waiting for transfers between devices  2.28 us (2%)
    all_gather x3, blocking collectives, prefix_2(): gathered = jax.tree.map(lambda a: lax.all_gather(a, axis), part)  32.7 us
    another operation x2, loops' own time, prefix_2(): return lax.fori_loop(0, place, one, state)  19.2 us
    unnamed x1, blocking collectives  19 us
    ppermute x1, starting transfers between devices, padded_2(): lax.ppermute(lax.slice_in_dim(block, block.shape[dim] - width, None, axis...  7.32 us
    unnamed x16, local copies, waits for them, and re-layouts  5.46 us
    dynamic_slice x12, local copies, waits for them, and re-layouts, one(): lax.dynamic_index_in_dim(a, hop, 0, False)  3.97 us
    dot_general x1, matrix products, on_device(): passone = strain_rate - jnp.dot(smooth_one, strain_rate, precision=precise)  3.83 us
  transfers between devices with their start and end apart: 2, of which 1 were waited for; matrix products, arithmetic and copies ran while one was open for 1% of the time, Pallas kernels for 0%

commit v1 on v0

v1 whole, which is shorter than its diff:
```python
import functools

import jax
import jax.numpy as jnp
import ml_dtypes
import numpy as np
from jax import lax
from jax.experimental import pallas as pl
from jax.experimental.pallas import tpu as pltpu
from jax.sharding import PartitionSpec as P

LONGEST = 2048
F32 = jnp.float32
BF16 = jnp.bfloat16


def split_np(a):
    hi = a.astype(ml_dtypes.bfloat16)
    lo = (a - hi.astype(np.float64)).astype(ml_dtypes.bfloat16)
    return hi, lo


def time_constants(slab, part):
    p1 = 1.0 - 1.0 / (2.0 * slab)
    p2 = 1.0 - 1.0 / (8.0 * slab)
    gain = 1.0 / (8.0 * slab) ** 0.5
    k = np.arange(part, dtype=np.float64)
    off = k[:, None] - k[None, :]
    low = off >= 0
    safe = np.maximum(off, 0.0)
    g1 = np.where(low, (1.0 - p1) * p1**safe, 0.0)
    g2 = np.where(low, (1.0 - p2) * p2**safe, 0.0)
    one = np.eye(part)
    pass1 = one - g1
    low2 = g2 @ pass1
    filt = pass1 - low2
    integ = gain * np.cumsum(filt, axis=0)
    d1 = p1 ** (k + 1.0)
    d2 = p2 ** (k + 1.0)
    r1 = d1 - g2 @ d1
    c1 = gain * np.cumsum(r1)
    c2 = gain * np.cumsum(d2)
    rest = one - filt
    ends = np.stack([g1[-1], low2[-1], integ[-1]])
    trans = np.array(
        [[d1[-1], 0.0, 0.0], [r1[-1] - d1[-1], d2[-1], 0.0], [-c1[-1], -c2[-1], 1.0]]
    )
    strain_of = np.stack([-c1, -c2, np.ones(part)], axis=1)
    filt_of = np.stack([-r1, -d2, np.zeros(part)], axis=1)
    mats = np.stack([*split_np(integ), *split_np(rest)])
    e_hi, e_lo = split_np(ends)
    e_rows = np.zeros((16, part), ml_dtypes.bfloat16)
    e_rows[0:3], e_rows[3:6] = e_hi, e_lo
    cols = np.zeros((2, part, 16), ml_dtypes.bfloat16)
    for n, c in enumerate((strain_of, filt_of)):
        hi, lo = split_np(c)
        cols[n, :, 0:3], cols[n, :, 3:6], cols[n, :, 6:9] = hi, lo, hi
    return mats, e_rows, cols, trans


def split(a):
    hi = a.astype(BF16)
    return hi, (a - hi.astype(F32)).astype(BF16)


def mm(a, b):
    return jnp.dot(a, b, preferred_element_type=F32)


def kernel(
    n_chan, n_tm, reach, trans,
    x_hbm, gauge_hbm, valid_hbm, seg_hbm, sten_hbm, mats_hbm, ends_hbm, cols_hbm,
    strain_hbm, vel_hbm,
    x, gauge, valid, seg, sten, mats, ends, cols,
    xh, xl, vh, vl, u, strain, vel,
    right_out, left_out, right_in, left_in, state_out, state_in, st_rows,
    in_sem, out_sem, right_send, right_recv, left_send, left_recv, st_send, st_recv,
):
    slab, width = x.shape
    part = mats.shape[1]
    parts = slab // part
    tiles = width // 128
    ttiles = slab // 128
    j = lax.axis_index("chan")
    i = lax.axis_index("tm")

    blank = jnp.where(lax.broadcasted_iota(jnp.int32, (ttiles + 4, 128), 0) < ttiles, 0.0, -1.0)
    for d in range(reach):
        right_in[d] = blank
    left_in[...] = blank
    for d in range(n_tm - 1):
        state_in[d] = jnp.zeros((8, width), F32)

    barrier = pltpu.get_barrier_semaphore()
    for d in range(reach):
        @pl.when(j > d)
        def _():
            pl.semaphore_signal(barrier, inc=1, device_id={"chan": j - 1 - d, "tm": i})
    @pl.when(j < n_chan - 1)
    def _():
        pl.semaphore_signal(barrier, inc=1, device_id={"chan": j + 1, "tm": i})
    for d in range(n_tm - 1):
        @pl.when(i > d)
        def _():
            pl.semaphore_signal(barrier, inc=1, device_id={"chan": j, "tm": i - 1 - d})

    loads = [
        pltpu.make_async_copy(src, dst, in_sem.at[n])
        for n, (src, dst) in enumerate(
            [(gauge_hbm, gauge), (valid_hbm, valid), (seg_hbm, seg), (sten_hbm, sten),
             (x_hbm, x), (ends_hbm, ends), (cols_hbm, cols), (mats_hbm, mats)]
        )
    ]
    for c in loads:
        c.start()
    for c in loads[:4]:
        c.wait()

    ids = seg[...].astype(F32)
    w = gauge[...] * valid[...].astype(F32)
    lane = lax.broadcasted_iota(jnp.int32, (1, width), 1)
    tail = ids[:, width - 1:width]
    head = ids[:, 0:1]
    w_tail = jnp.where(ids == tail, w, 0.0)
    s0, s1 = sten[0:1, :], sten[1:2, :]
    s2_all = sten[2:3, :]
    s2 = jnp.where(lane == width - 1, 0.0, s2_all)
    edge = jnp.where(lane == width - 1, s2_all, 0.0)
    ids_prev = pltpu.roll(ids, 1, 1)
    ids_next = pltpu.roll(ids, width - 1, 1)

    def column(row):
        return jnp.transpose(jnp.broadcast_to(row, (128, 128)))

    def wide(block):
        return jnp.concatenate([block] * tiles, axis=1)

    for q in range(tiles):
        span = slice(q * 128, (q + 1) * 128)
        idc = wide(column(ids[:, span]))
        wc = wide(column(w[:, span]))
        gap = lax.broadcasted_iota(jnp.int32, (128, width), 1) - (
            lax.broadcasted_iota(jnp.int32, (128, width), 0) + q * 128
        )
        v = jnp.where((gap >= 1) & (idc == ids_prev), s0, 0.0)
        v = v + jnp.where((gap >= 0) & (idc == ids), s1, 0.0)
        v = v + jnp.where((gap >= -1) & (idc == ids_next), s2, 0.0)
        hi, lo = split(v * wc)
        vh[span, :] = hi
        vl[span, :] = lo

    loads[4].wait()
    eye = lax.broadcasted_iota(jnp.int32, (128, 128), 0) == lax.broadcasted_iota(
        jnp.int32, (128, 128), 1
    )
    w_first = w[:, 0:1]
    y = []
    for q in range(ttiles):
        span = slice(q * 128, (q + 1) * 128)
        block = x[span, :]
        yq = jnp.sum(block * w_tail, axis=1, keepdims=True)
        y.append(yq)
        right_out[q:q + 1, :] = jnp.sum(jnp.where(eye, yq, 0.0), axis=0, keepdims=True)
        left_out[q:q + 1, :] = jnp.sum(
            jnp.where(eye, block[:, 0:1] * w_first, 0.0), axis=0, keepdims=True
        )
    right_out[ttiles:, :] = jnp.broadcast_to(tail, (4, 128))
    left_out[ttiles:, :] = jnp.broadcast_to(head, (4, 128))

    targets = (
        jnp.minimum(reach, n_chan - 1 - j) + jnp.minimum(j, 1) + jnp.minimum(n_tm - 1, n_tm - 1 - i)
    )
    pl.semaphore_wait(barrier, targets)

    def to_right(d):
        return pltpu.make_async_remote_copy(
            right_out, right_in.at[d], right_send.at[d], right_recv.at[d],
            device_id={"chan": j + 1 + d, "tm": i},
        )

    def to_left():
        return pltpu.make_async_remote_copy(
            left_out, left_in, left_send, left_recv, device_id={"chan": j - 1, "tm": i}
        )

    def to_later(d):
        return pltpu.make_async_remote_copy(
            state_out, state_in.at[d], st_send.at[d], st_recv.at[d],
            device_id={"chan": j, "tm": i + 1 + d},
        )

    for d in range(reach):
        @pl.when(j + 1 + d < n_chan)
        def _():
            to_right(d).start()
    @pl.when(j > 0)
    def _():
        to_left().start()

    loads[5].wait()
    ends_x = []
    for k in range(parts):
        rows = slice(k * part, (k + 1) * part)
        hi, lo = split(x[rows, :])
        xh[rows, :] = hi
        xl[rows, :] = lo
        u[rows, :] = mm(hi, vh[...]) + mm(lo, vh[...]) + mm(hi, vl[...])
        e = mm(ends[...], hi) + mm(ends[...], lo)
        ends_x.append(e[0:3] + e[3:6])

    for d in range(reach):
        @pl.when(j > d)
        def _():
            to_right(d).wait_recv()
    @pl.when(j < n_chan - 1)
    def _():
        to_left().wait_recv()

    first = right_in[0]
    tail_prev = first[ttiles:ttiles + 1, :]
    carry = first[0:ttiles]
    for d in range(1, reach):
        far = right_in[d]
        carry = carry + jnp.where(far[ttiles:ttiles + 1, :] == tail_prev, far[0:ttiles], 0.0)
    beyond = left_in[...]
    tail_ids = jnp.concatenate([tail_prev] * tiles, axis=1)
    m = jnp.where(ids == tail_ids, 1.0, 0.0)
    m_prev = jnp.where(lane == 0, 1.0, pltpu.roll(m, 1, 1))
    m_next = pltpu.roll(m, width - 1, 1)
    a = s0 * m_prev + s1 * m + s2 * m_next
    m_tail = m[:, width - 1:width]
    same = jnp.where(beyond[ttiles:ttiles + 1, :] == tail, 1.0, 0.0)
    past = beyond[0:ttiles] + same * (right_out[0:ttiles, :] + m_tail * carry)
    for q in range(ttiles):
        span = slice(q * 128, (q + 1) * 128)
        cc = wide(column(carry[q:q + 1, :]))
        pc = column(past[q:q + 1, :])
        u[span, :] = u[span, :] + cc * a
        u[span, width - 128:] = u[span, width - 128:] + pc * edge[:, width - 128:]

    ends_u = []
    halves = []
    for k in range(parts):
        rows = slice(k * part, (k + 1) * part)
        hi, lo = split(u[rows, :])
        e = mm(ends[...], hi) + mm(ends[...], lo)
        ends_u.append(e[0:3] + e[3:6])
        halves.append((hi, lo))

    def combine(rows, coef):
        return [
            functools.reduce(
                lambda p, r: p + r,
                [float(coef[n, o]) * rows[o] for o in range(3) if coef[n, o] != 0.0],
            )
            for n in range(3)
        ]

    def rows_of(e):
        return [e[n:n + 1] for n in range(3)]

    def fold(list_of_ends):
        total = rows_of(list_of_ends[0])
        for e in list_of_ends[1:]:
            total = [p + r for p, r in zip(combine(total, trans), rows_of(e))]
        return total

    end_x, end_u = fold(ends_x), fold(ends_u)
    for n in range(3):
        state_out[n:n + 1, :] = end_x[n]
    for n in range(2):
        state_out[3 + n:4 + n, :] = end_u[n]
    state_out[5:8, :] = jnp.zeros((3, width), F32)

    for d in range(n_tm - 1):
        @pl.when(i + 1 + d < n_tm)
        def _():
            to_later(d).start()

    loads[6].wait()
    loads[7].wait()
    for k in range(parts):
        rows = slice(k * part, (k + 1) * part)
        strain[rows, :] = (
            mm(mats[0], xh[rows, :]) + mm(mats[0], xl[rows, :]) + mm(mats[1], xh[rows, :])
        )
        hi, lo = halves[k]
        vel[rows, :] = u[rows, :] - (mm(mats[2], hi) + mm(mats[2], lo) + mm(mats[3], hi))

    for d in range(n_tm - 1):
        @pl.when(i > d)
        def _():
            to_later(d).wait_recv()

    step = np.linalg.matrix_power(trans, parts)
    now_x = [jnp.zeros((1, width), F32)] * 3
    now_u = [jnp.zeros((1, width), F32)] * 3
    power = np.eye(3)
    for d in range(n_tm - 1):
        got = state_in[d]
        add_x = combine([got[n:n + 1] for n in range(3)], power)
        add_u = combine([got[3:4], got[4:5], jnp.zeros((1, width), F32)], power)
        now_x = [p + r for p, r in zip(now_x, add_x)]
        now_u = [p + r for p, r in zip(now_u, add_u)]
        power = step @ power

    st_rows[...] = jnp.zeros_like(st_rows)
    stores = []
    for k in range(parts):
        rows = slice(k * part, (k + 1) * part)
        for n, (now, dst, out) in enumerate(((now_x, strain, strain_hbm), (now_u, vel, vel_hbm))):
            slot = 2 * k + n
            for r in range(3):
                hi = now[r].astype(BF16).astype(F32)
                st_rows[slot, r:r + 1, :] = hi
                st_rows[slot, 3 + r:4 + r, :] = hi
                st_rows[slot, 6 + r:7 + r, :] = now[r] - hi
            dst[rows, :] = dst[rows, :] + mm(cols[n], st_rows[slot].astype(BF16))
            copy = pltpu.make_async_copy(dst.at[rows, :], out.at[rows, :], out_sem.at[slot])
            copy.start()
            stores.append(copy)
        if k + 1 < parts:
            now_x = [p + r for p, r in zip(combine(now_x, trans), rows_of(ends_x[k]))]
            now_u = [p + r for p, r in zip(combine(now_u, trans), rows_of(ends_u[k]))]

    for d in range(reach):
        @pl.when(j + 1 + d < n_chan)
        def _():
            to_right(d).wait_send()
    @pl.when(j > 0)
    def _():
        to_left().wait_send()
    for d in range(n_tm - 1):
        @pl.when(i + 1 + d < n_tm)
        def _():
            to_later(d).wait_send()
    for c in stores:
        c.wait()


def on_device(n_chan, n_tm, strain_rate, gauge, valid, segment, stencil):
    slab, width = strain_rate.shape
    part = 256 if slab % 256 == 0 else 128
    parts = slab // part
    reach = min(n_chan - 1, -(-LONGEST // width))
    mats, ends, cols, trans = time_constants(slab, part)
    ttiles = slab // 128
    any_spec = pl.BlockSpec(memory_space=pl.ANY)
    out = jax.ShapeDtypeStruct((slab, width), F32)
    return pl.pallas_call(
        functools.partial(kernel, n_chan, n_tm, reach, trans),
        out_shape=(out, out),
        in_specs=[any_spec] * 8,
        out_specs=(any_spec, any_spec),
        scratch_shapes=[
            pltpu.VMEM((slab, width), F32),
            pltpu.VMEM((1, width), F32),
            pltpu.VMEM((1, width), jnp.int32),
            pltpu.VMEM((1, width), jnp.int32),
            pltpu.VMEM((3, width), F32),
            pltpu.VMEM(mats.shape, BF16),
            pltpu.VMEM(ends.shape, BF16),
            pltpu.VMEM(cols.shape, BF16),
            pltpu.VMEM((slab, width), BF16),
            pltpu.VMEM((slab, width), BF16),
            pltpu.VMEM((width, width), BF16),
            pltpu.VMEM((width, width), BF16),
            pltpu.VMEM((slab, width), F32),
            pltpu.VMEM((slab, width), F32),
            pltpu.VMEM((slab, width), F32),
            pltpu.VMEM((ttiles + 4, 128), F32),
            pltpu.VMEM((ttiles + 4, 128), F32),
            pltpu.VMEM((reach, ttiles + 4, 128), F32),
            pltpu.VMEM((ttiles + 4, 128), F32),
            pltpu.VMEM((8, width), F32),
            pltpu.VMEM((n_tm - 1, 8, width), F32),
            pltpu.VMEM((2 * parts, 16, width), F32),
            pltpu.SemaphoreType.DMA((8,)),
            pltpu.SemaphoreType.DMA((2 * parts,)),
            pltpu.SemaphoreType.DMA((reach,)),
            pltpu.SemaphoreType.DMA((reach,)),
            pltpu.SemaphoreType.DMA,
            pltpu.SemaphoreType.DMA,
            pltpu.SemaphoreType.DMA((n_tm - 1,)),
            pltpu.SemaphoreType.DMA((n_tm - 1,)),
        ],
        compiler_params=pltpu.CompilerParams(
            collective_id=0, has_side_effects=True, vmem_limit_bytes=62 * 1024 * 1024
        ),
    )(
        strain_rate, gauge[None, :], valid[None, :], segment[None, :], stencil,
        jnp.asarray(mats), jnp.asarray(ends), jnp.asarray(cols),
    )


def solution(mesh):
    in_specs = (P("tm", "chan"), P("chan"), P("chan"), P("chan"), P(None, "chan"))
    out_specs = (P("tm", "chan"), P("tm", "chan"))
    return jax.shard_map(
        functools.partial(on_device, mesh.shape["chan"], mesh.shape["tm"]),
        mesh=mesh, in_specs=in_specs, out_specs=out_specs, check_vma=False,
    )
```

time: 119 us -> 14.7 us (0.12)
  the two profiles are of different devices: /device:TPU:26 before, /device:TPU:0 now
where the time goes in v1:
time: 14.7 us; the launch traced here: 14.4 us
  Pallas kernels  10.5 us (71%)
  local copies, waits for them, and re-layouts  3.32 us (23%)
  between operations  0.65 us (4%)
    pallas_call x1, Pallas kernels, on_device(): pl.pallas_call(functools.partial(kernel, n_chan, n_tm, reach, trans), out...  10.5 us
    unnamed x4, local copies, waits for them, and re-layouts  3.32 us

profile of v1, /device:TPU:0, one launch (start us, length us, event | category | flops | bytes accessed | tf_op | source)
XLA Modules:
  0.0 14.4 jit_solution(4847614749199397557)
XLA Ops:
  0.6 10.5 %shard_map.95 = (f32[512,512]{1,0:T(8,128)}, f32[512,512]{1,0:T(8,128)}) custom-call(f32[512,512]{1,0:T(8,128)} %x_hbm.1, f32[1,512]{1,0:T(1,128)} %bitcast.3, s32[1,512]{1,0:T(1,128)} %bitcast.4, s32[1,512]{1,0:T(1,128)} %bitcast.5, f32[3,512]{1,0:T(4,128)} %sten_hbm.1, bf16[4,256,256]{2,1,0:T(8,128)(2,1)} %constant.6.clone.mats_hbm, ...), custom_call_target="tpu_custom_call" | custom-call | tf_op jit(solution)/shard_map/pallas_call | solution.py:350
  11.1 0.0 copy-start
  11.1 2.4 %copy.12 = f32[512,512]{1,0:T(8,128)} copy(f32[512,512]{1,0:T(8,128)} %get-tuple-element.4) | data formatting | bytes 2097152
  13.5 0.0 copy-done
  13.5 1.0 %copy.13 = f32[512,512]{1,0:T(8,128)} copy(f32[512,512]{1,0:T(8,128)S(1)} %copy-done) | data formatting | bytes 2097152
Async XLA Ops:
  11.1 2.4 %copy-start = (f32[512,512]{1,0:T(8,128)S(1)}, f32[512,512]{1,0:T(8,128)}, u32[]{:S(2)}) copy-start(f32[512,512]{1,0:T(8,128)} %get-tuple-element.5) | copy-start | bytes 3145732

commit v2 on v1

--- a/solution.py
+++ b/solution.py
@@ -55,7 +55,8 @@
     for n, c in enumerate((strain_of, filt_of)):
         hi, lo = split_np(c)
         cols[n, :, 0:3], cols[n, :, 3:6], cols[n, :, 6:9] = hi, lo, hi
-    return mats, e_rows, cols, trans
+    e_tiles = np.tile(ends.astype(np.float32).reshape(3, part // 128, 128), (1, slab // part, 1))
+    return mats, e_rows, cols, trans, e_tiles
 
 
 def split(a):
@@ -69,12 +70,12 @@
 
 def kernel(
     n_chan, n_tm, reach, trans,
-    x_hbm, gauge_hbm, valid_hbm, seg_hbm, sten_hbm, mats_hbm, ends_hbm, cols_hbm,
-    strain_hbm, vel_hbm,
-    x, gauge, valid, seg, sten, mats, ends, cols,
-    xh, xl, vh, vl, u, strain, vel,
-    right_out, left_out, right_in, left_in, state_out, state_in, st_rows,
-    in_sem, out_sem, right_send, right_recv, left_send, left_recv, st_send, st_recv,
+    x_hbm, gauge_hbm, valid_hbm, seg_hbm, sten_hbm, mats_hbm, ends_hbm, tiles_hbm,
+    strain, vel, st_rows,
+    x, gauge, valid, seg, sten, mats, ends, e_tiles,
+    xh, xl, vh, vl, u,
+    right_out, left_out, right_in, left_in, state_out, state_in,
+    in_sem, right_send, right_recv, left_send, left_recv, st_send, st_recv,
 ):
     slab, width = x.shape
     part = mats.shape[1]
@@ -108,7 +109,7 @@
         pltpu.make_async_copy(src, dst, in_sem.at[n])
         for n, (src, dst) in enumerate(
             [(gauge_hbm, gauge), (valid_hbm, valid), (seg_hbm, seg), (sten_hbm, sten),
-             (x_hbm, x), (ends_hbm, ends), (cols_hbm, cols), (mats_hbm, mats)]
+             (x_hbm, x), (ends_hbm, ends), (tiles_hbm, e_tiles), (mats_hbm, mats)]
         )
     ]
     for c in loads:
@@ -134,20 +135,6 @@
 
     def wide(block):
         return jnp.concatenate([block] * tiles, axis=1)
-
-    for q in range(tiles):
-        span = slice(q * 128, (q + 1) * 128)
-        idc = wide(column(ids[:, span]))
-        wc = wide(column(w[:, span]))
-        gap = lax.broadcasted_iota(jnp.int32, (128, width), 1) - (
-            lax.broadcasted_iota(jnp.int32, (128, width), 0) + q * 128
-        )
-        v = jnp.where((gap >= 1) & (idc == ids_prev), s0, 0.0)
-        v = v + jnp.where((gap >= 0) & (idc == ids), s1, 0.0)
-        v = v + jnp.where((gap >= -1) & (idc == ids_next), s2, 0.0)
-        hi, lo = split(v * wc)
-        vh[span, :] = hi
-        vl[span, :] = lo
 
     loads[4].wait()
     eye = lax.broadcasted_iota(jnp.int32, (128, 128), 0) == lax.broadcasted_iota(
@@ -197,8 +184,22 @@
     def _():
         to_left().start()
 
+    for q in range(tiles):
+        span = slice(q * 128, (q + 1) * 128)
+        idc = wide(column(ids[:, span]))
+        wc = wide(column(w[:, span]))
+        gap = lax.broadcasted_iota(jnp.int32, (128, width), 1) - (
+            lax.broadcasted_iota(jnp.int32, (128, width), 0) + q * 128
+        )
+        v = jnp.where((gap >= 1) & (idc == ids_prev), s0, 0.0)
+        v = v + jnp.where((gap >= 0) & (idc == ids), s1, 0.0)
+        v = v + jnp.where((gap >= -1) & (idc == ids_next), s2, 0.0)
+        hi, lo = split(v * wc)
+        vh[span, :] = hi
+        vl[span, :] = lo
+
     loads[5].wait()
-    ends_x = []
+    ends_x, ends_u = [], []
     for k in range(parts):
         rows = slice(k * part, (k + 1) * part)
         hi, lo = split(x[rows, :])
@@ -207,6 +208,10 @@
         u[rows, :] = mm(hi, vh[...]) + mm(lo, vh[...]) + mm(hi, vl[...])
         e = mm(ends[...], hi) + mm(ends[...], lo)
         ends_x.append(e[0:3] + e[3:6])
+        hi, lo = split(u[rows, :])
+        e = mm(ends[...], hi) + mm(ends[...], lo)
+        ends_u.append(e[0:3] + e[3:6])
+    loads[6].wait()
 
     for d in range(reach):
         @pl.when(j > d)
@@ -231,21 +236,19 @@
     m_tail = m[:, width - 1:width]
     same = jnp.where(beyond[ttiles:ttiles + 1, :] == tail, 1.0, 0.0)
     past = beyond[0:ttiles] + same * (right_out[0:ttiles, :] + m_tail * carry)
-    for q in range(ttiles):
-        span = slice(q * 128, (q + 1) * 128)
-        cc = wide(column(carry[q:q + 1, :]))
-        pc = column(past[q:q + 1, :])
-        u[span, :] = u[span, :] + cc * a
-        u[span, width - 128:] = u[span, width - 128:] + pc * edge[:, width - 128:]
-
-    ends_u = []
-    halves = []
-    for k in range(parts):
-        rows = slice(k * part, (k + 1) * part)
-        hi, lo = split(u[rows, :])
-        e = mm(ends[...], hi) + mm(ends[...], lo)
-        ends_u.append(e[0:3] + e[3:6])
-        halves.append((hi, lo))
+    per = part // 128
+    for n in range(2):
+        of_carry = jnp.sum(carry * e_tiles[n], axis=1, keepdims=True)
+        of_past = jnp.sum(past * e_tiles[n], axis=1, keepdims=True)
+        for k in range(parts):
+            span = slice(k * per, (k + 1) * per)
+            more = (
+                jnp.sum(of_carry[span], axis=0, keepdims=True) * a
+                + jnp.sum(of_past[span], axis=0, keepdims=True) * edge
+            )
+            ends_u[k] = ends_u[k] + jnp.where(
+                lax.broadcasted_iota(jnp.int32, (3, width), 0) == n, more, 0.0
+            )
 
     def combine(rows, coef):
         return [
@@ -277,14 +280,20 @@
         def _():
             to_later(d).start()
 
-    loads[6].wait()
+    for q in range(ttiles):
+        span = slice(q * 128, (q + 1) * 128)
+        cc = wide(column(carry[q:q + 1, :]))
+        pc = column(past[q:q + 1, :])
+        u[span, :] = u[span, :] + cc * a
+        u[span, width - 128:] = u[span, width - 128:] + pc * edge[:, width - 128:]
+
     loads[7].wait()
     for k in range(parts):
         rows = slice(k * part, (k + 1) * part)
         strain[rows, :] = (
             mm(mats[0], xh[rows, :]) + mm(mats[0], xl[rows, :]) + mm(mats[1], xh[rows, :])
         )
-        hi, lo = halves[k]
+        hi, lo = split(u[rows, :])
         vel[rows, :] = u[rows, :] - (mm(mats[2], hi) + mm(mats[2], lo) + mm(mats[3], hi))
 
     for d in range(n_tm - 1):
@@ -305,20 +314,13 @@
         power = step @ power
 
     st_rows[...] = jnp.zeros_like(st_rows)
-    stores = []
     for k in range(parts):
-        rows = slice(k * part, (k + 1) * part)
-        for n, (now, dst, out) in enumerate(((now_x, strain, strain_hbm), (now_u, vel, vel_hbm))):
-            slot = 2 * k + n
+        for n, now in enumerate((now_x, now_u)):
             for r in range(3):
                 hi = now[r].astype(BF16).astype(F32)
-                st_rows[slot, r:r + 1, :] = hi
-                st_rows[slot, 3 + r:4 + r, :] = hi
-                st_rows[slot, 6 + r:7 + r, :] = now[r] - hi
-            dst[rows, :] = dst[rows, :] + mm(cols[n], st_rows[slot].astype(BF16))
-            copy = pltpu.make_async_copy(dst.at[rows, :], out.at[rows, :], out_sem.at[slot])
-            copy.start()
-            stores.append(copy)
+                st_rows[2 * k + n, r:r + 1, :] = hi
+                st_rows[2 * k + n, 3 + r:4 + r, :] = hi
+                st_rows[2 * k + n, 6 + r:7 + r, :] = now[r] - hi
         if k + 1 < parts:
             now_x = [p + r for p, r in zip(combine(now_x, trans), rows_of(ends_x[k]))]
             now_u = [p + r for p, r in zip(combine(now_u, trans), rows_of(ends_u[k]))]
@@ -334,6 +336,20 @@
         @pl.when(i + 1 + d < n_tm)
         def _():
             to_later(d).wait_send()
+
+
+def finish(strain, vel, st_rows, cols, strain_hbm, vel_hbm, buf, out_sem):
+    slab = strain.shape[0]
+    part = cols.shape[1]
+    stores = []
+    for k in range(slab // part):
+        rows = slice(k * part, (k + 1) * part)
+        for n, (src, out) in enumerate(((strain, strain_hbm), (vel, vel_hbm))):
+            slot = 2 * k + n
+            buf[slot] = src[rows, :] + mm(cols[n], st_rows[slot].astype(BF16))
+            copy = pltpu.make_async_copy(buf.at[slot], out.at[rows, :], out_sem.at[slot])
+            copy.start()
+            stores.append(copy)
     for c in stores:
         c.wait()
 
@@ -343,15 +359,21 @@
     part = 256 if slab % 256 == 0 else 128
     parts = slab // part
     reach = min(n_chan - 1, -(-LONGEST // width))
-    mats, ends, cols, trans = time_constants(slab, part)
+    mats, ends, cols, trans, e_tiles = time_constants(slab, part)
     ttiles = slab // 128
+    hbm = pl.BlockSpec(memory_space=pltpu.HBM)
     any_spec = pl.BlockSpec(memory_space=pl.ANY)
+    local = pl.BlockSpec(memory_space=pltpu.VMEM)
     out = jax.ShapeDtypeStruct((slab, width), F32)
-    return pl.pallas_call(
+    strain, vel, st_rows = pl.pallas_call(
         functools.partial(kernel, n_chan, n_tm, reach, trans),
-        out_shape=(out, out),
-        in_specs=[any_spec] * 8,
-        out_specs=(any_spec, any_spec),
+        out_shape=(
+            pltpu.VMEM((slab, width), F32),
+            pltpu.VMEM((slab, width), F32),
+            pltpu.VMEM((2 * parts, 16, width), F32),
+        ),
+        in_specs=[hbm] * 8,
+        out_specs=(local, local, local),
         scratch_shapes=[
             pltpu.VMEM((slab, width), F32),
             pltpu.VMEM((1, width), F32),
@@ -360,13 +382,11 @@
             pltpu.VMEM((3, width), F32),
             pltpu.VMEM(mats.shape, BF16),
             pltpu.VMEM(ends.shape, BF16),
-            pltpu.VMEM(cols.shape, BF16),
+            pltpu.VMEM(e_tiles.shape, F32),
             pltpu.VMEM((slab, width), BF16),
             pltpu.VMEM((slab, width), BF16),
             pltpu.VMEM((width, width), BF16),
             pltpu.VMEM((width, width), BF16),
-            pltpu.VMEM((slab, width), F32),
-            pltpu.VMEM((slab, width), F32),
             pltpu.VMEM((slab, width), F32),
             pltpu.VMEM((ttiles + 4, 128), F32),
             pltpu.VMEM((ttiles + 4, 128), F32),
@@ -374,9 +394,7 @@
             pltpu.VMEM((ttiles + 4, 128), F32),
             pltpu.VMEM((8, width), F32),
             pltpu.VMEM((n_tm - 1, 8, width), F32),
-            pltpu.VMEM((2 * parts, 16, width), F32),
             pltpu.SemaphoreType.DMA((8,)),
-            pltpu.SemaphoreType.DMA((2 * parts,)),
             pltpu.SemaphoreType.DMA((reach,)),
             pltpu.SemaphoreType.DMA((reach,)),
             pltpu.SemaphoreType.DMA,
@@ -385,12 +403,28 @@
             pltpu.SemaphoreType.DMA((n_tm - 1,)),
         ],
         compiler_params=pltpu.CompilerParams(
-            collective_id=0, has_side_effects=True, vmem_limit_bytes=62 * 1024 * 1024
+            collective_id=0, has_side_effects=True, vmem_limit_bytes=32 * 1024 * 1024
         ),
     )(
-        strain_rate, gauge[None, :], valid[None, :], segment[None, :], stencil,
-        jnp.asarray(mats), jnp.asarray(ends), jnp.asarray(cols),
+        *[
+            pltpu.with_memory_space_constraint(a, pltpu.HBM)
+            for a in (
+                strain_rate, gauge[None, :], valid[None, :], segment[None, :], stencil,
+                jnp.asarray(mats), jnp.asarray(ends), jnp.asarray(e_tiles),
+            )
+        ],
     )
+    return pl.pallas_call(
+        finish,
+        out_shape=(out, out),
+        in_specs=[local] * 4,
+        out_specs=(any_spec, any_spec),
+        scratch_shapes=[
+            pltpu.VMEM((2 * parts, part, width), F32),
+            pltpu.SemaphoreType.DMA((2 * parts,)),
+        ],
+        compiler_params=pltpu.CompilerParams(vmem_limit_bytes=16 * 1024 * 1024),
+    )(strain, vel, st_rows, jnp.asarray(cols))
 
 
 def solution(mesh):

time: 14.7 us -> 11.9 us (0.81)
  local copies, waits for them, and re-layouts: 3.32 us -> 0.01 us
  Pallas kernels: 10.5 us -> 11.1 us
    unnamed x4 -> x2, local copies, waits for them, and re-layouts: 3.32 us -> 0.01 us
    pallas_call x0 -> x1, Pallas kernels: none -> 1.55 us  [on_device(): pl.pallas_call(finish, out_shape=(out, out), in_specs=[local] * 4, out_sp...]
    pallas_call x1, Pallas kernels: 10.5 us -> 9.55 us  [on_device(): pl.pallas_call(functools.partial(kernel, n_chan, n_tm, reach, trans), out...]
where the time goes in v2:
time: 11.9 us; the launch traced here: 11.8 us
  Pallas kernels  11.1 us (93%)
  between operations  0.65 us (5%)
    pallas_call x1, Pallas kernels, on_device(): pl.pallas_call(functools.partial(kernel, n_chan, n_tm, reach, trans), out...  9.55 us
    pallas_call x1, Pallas kernels, on_device(): pl.pallas_call(finish, out_shape=(out, out), in_specs=[local] * 4, out_sp...  1.55 us

profile of v2, /device:TPU:0, one launch (start us, length us, event | category | flops | bytes accessed | tf_op | source)
XLA Modules:
  0.0 11.8 jit_solution(5915012302150483631)
XLA Ops:
  0.6 0.0 copy-start
  0.6 9.5 %shard_map.104 = (f32[512,512]{1,0:T(8,128)S(1)}, f32[512,512]{1,0:T(8,128)S(1)}, f32[4,16,512]{2,1,0:T(8,128)S(1)}) custom-call(f32[512,512]{1,0:T(8,128)} %x_hbm.1, f32[1,512]{1,0:T(1,128)} %bitcast.3, s32[1,512]{1,0:T(1,128)} %bitcast.4, s32[1,512]{1,0:T(1,128)} %bitcast.5, f32[3,512]{1,0:T(4,128)} %sten_hbm.1, ...), custom_call_target="tpu_custom_call" | custom-call | tf_op jit(solution)/shard_map/pallas_call | solution.py:368
  10.2 0.0 copy-done
  10.2 1.5 %shard_map.105 = (f32[512,512]{1,0:T(8,128)}, f32[512,512]{1,0:T(8,128)}) custom-call(f32[512,512]{1,0:T(8,128)S(1)} %get-tuple-element.5.strain, f32[512,512]{1,0:T(8,128)S(1)} %get-tuple-element.6.vel, f32[4,16,512]{2,1,0:T(8,128)S(1)} %get-tuple-element.7.st_rows, bf16[2,256,16]{2,1,0:T(8,128)(2,1)S(1)} %copy-done), custom_call_target="tpu_custom_call" | custom-call | tf_op jit(solution)/shard_map/pallas_call | solution.py:417
Async XLA Ops:
  0.6 9.6 %copy-start = (bf16[2,256,16]{2,1,0:T(8,128)(2,1)S(1)}, bf16[2,256,16]{2,1,0:T(8,128)(2,1)}, u32[]{:S(2)}) copy-start(bf16[2,256,16]{2,1,0:T(8,128)(2,1)} %constant.11.clone.cols) | copy-start | bytes 49156

commit v3 on v2

--- a/solution.py
+++ b/solution.py
@@ -51,10 +51,10 @@
     e_hi, e_lo = split_np(ends)
     e_rows = np.zeros((16, part), ml_dtypes.bfloat16)
     e_rows[0:3], e_rows[3:6] = e_hi, e_lo
-    cols = np.zeros((2, part, 16), ml_dtypes.bfloat16)
+    cols = np.zeros((2, 16, part), np.float32)
     for n, c in enumerate((strain_of, filt_of)):
         hi, lo = split_np(c)
-        cols[n, :, 0:3], cols[n, :, 3:6], cols[n, :, 6:9] = hi, lo, hi
+        cols[n, 0:3], cols[n, 3:6], cols[n, 6:9] = hi.T, lo.T, hi.T
     e_tiles = np.tile(ends.astype(np.float32).reshape(3, part // 128, 128), (1, slab // part, 1))
     return mats, e_rows, cols, trans, e_tiles
 
@@ -64,16 +64,24 @@
     return hi, (a - hi.astype(F32)).astype(BF16)
 
 
+def mm_nt(a, b):
+    return lax.dot_general(a, b, (((1,), (1,)), ((), ())), preferred_element_type=F32)
+
+
+def mm_tn(a, b):
+    return lax.dot_general(a, b, (((0,), (0,)), ((), ())), preferred_element_type=F32)
+
+
 def mm(a, b):
     return jnp.dot(a, b, preferred_element_type=F32)
 
 
 def kernel(
     n_chan, n_tm, reach, trans,
-    x_hbm, gauge_hbm, valid_hbm, seg_hbm, sten_hbm, mats_hbm, ends_hbm, tiles_hbm,
-    strain, vel, st_rows,
-    x, gauge, valid, seg, sten, mats, ends, e_tiles,
-    xh, xl, vh, vl, u,
+    x_hbm, gauge_hbm, valid_hbm, seg_hbm, sten_hbm, mats_hbm, ends_hbm, tiles_hbm, cols_hbm,
+    strain, vel, st_rows, st_cols,
+    x, gauge, valid, seg, sten, mats, ends, e_tiles, cols,
+    xh, xl, vh, vl, pack,
     right_out, left_out, right_in, left_in, state_out, state_in,
     in_sem, right_send, right_recv, left_send, left_recv, st_send, st_recv,
 ):
@@ -109,10 +117,11 @@
         pltpu.make_async_copy(src, dst, in_sem.at[n])
         for n, (src, dst) in enumerate(
             [(gauge_hbm, gauge), (valid_hbm, valid), (seg_hbm, seg), (sten_hbm, sten),
-             (x_hbm, x), (ends_hbm, ends), (tiles_hbm, e_tiles), (mats_hbm, mats)]
+             (x_hbm, x), (ends_hbm, ends), (tiles_hbm, e_tiles), (cols_hbm, cols),
+             (mats_hbm, mats)]
         )
     ]
-    for c in loads:
+    for c in loads[:8]:
         c.start()
     for c in loads[:4]:
         c.wait()
@@ -136,7 +145,22 @@
     def wide(block):
         return jnp.concatenate([block] * tiles, axis=1)
 
+    for q in range(tiles):
+        span = slice(q * 128, (q + 1) * 128)
+        idc = wide(column(ids[:, span]))
+        wc = wide(column(w[:, span]))
+        gap = lax.broadcasted_iota(jnp.int32, (128, width), 1) - (
+            lax.broadcasted_iota(jnp.int32, (128, width), 0) + q * 128
+        )
+        v = jnp.where((gap >= 1) & (idc == ids_prev), s0, 0.0)
+        v = v + jnp.where((gap >= 0) & (idc == ids), s1, 0.0)
+        v = v + jnp.where((gap >= -1) & (idc == ids_next), s2, 0.0)
+        hi, lo = split(v * wc)
+        vh[span, :] = hi
+        vl[span, :] = lo
+
     loads[4].wait()
+    loads[8].start()
     eye = lax.broadcasted_iota(jnp.int32, (128, 128), 0) == lax.broadcasted_iota(
         jnp.int32, (128, 128), 1
     )
@@ -154,6 +178,18 @@
     right_out[ttiles:, :] = jnp.broadcast_to(tail, (4, 128))
     left_out[ttiles:, :] = jnp.broadcast_to(head, (4, 128))
 
+    for k in range(parts):
+        rows = slice(k * part, (k + 1) * part)
+        hi, lo = split(x[rows, :])
+        xh[rows, :] = hi
+        xl[rows, :] = lo
+    loads[8].wait()
+    for k in range(parts):
+        rows = slice(k * part, (k + 1) * part)
+        strain[rows, :] = (
+            mm(mats[0], xh[rows, :]) + mm(mats[0], xl[rows, :]) + mm(mats[1], xh[rows, :])
+        )
+
     targets = (
         jnp.minimum(reach, n_chan - 1 - j) + jnp.minimum(j, 1) + jnp.minimum(n_tm - 1, n_tm - 1 - i)
     )
@@ -184,34 +220,22 @@
     def _():
         to_left().start()
 
-    for q in range(tiles):
-        span = slice(q * 128, (q + 1) * 128)
-        idc = wide(column(ids[:, span]))
-        wc = wide(column(w[:, span]))
-        gap = lax.broadcasted_iota(jnp.int32, (128, width), 1) - (
-            lax.broadcasted_iota(jnp.int32, (128, width), 0) + q * 128
-        )
-        v = jnp.where((gap >= 1) & (idc == ids_prev), s0, 0.0)
-        v = v + jnp.where((gap >= 0) & (idc == ids), s1, 0.0)
-        v = v + jnp.where((gap >= -1) & (idc == ids_next), s2, 0.0)
-        hi, lo = split(v * wc)
-        vh[span, :] = hi
-        vl[span, :] = lo
-
-    loads[5].wait()
+    for c in loads[5:8]:
+        c.wait()
     ends_x, ends_u = [], []
+    pack[...] = jnp.zeros_like(pack)
     for k in range(parts):
         rows = slice(k * part, (k + 1) * part)
-        hi, lo = split(x[rows, :])
-        xh[rows, :] = hi
-        xl[rows, :] = lo
-        u[rows, :] = mm(hi, vh[...]) + mm(lo, vh[...]) + mm(hi, vl[...])
-        e = mm(ends[...], hi) + mm(ends[...], lo)
-        ends_x.append(e[0:3] + e[3:6])
-        hi, lo = split(u[rows, :])
-        e = mm(ends[...], hi) + mm(ends[...], lo)
-        ends_u.append(e[0:3] + e[3:6])
-    loads[6].wait()
+        e = mm(ends[...], xh[rows, :]) + mm(ends[...], xl[rows, :])
+        e = e[0:3] + e[3:6]
+        ends_x.append(e)
+        hi = e.astype(BF16).astype(F32)
+        pack[k, 0:3, :] = hi
+        pack[k, 8:11, :] = e - hi
+    for k in range(parts):
+        e = pack[k].astype(BF16)
+        e = mm(e, vh[...]) + mm(e, vl[...])
+        ends_u.append(e[0:3] + e[8:11])
 
     for d in range(reach):
         @pl.when(j > d)
@@ -280,21 +304,33 @@
         def _():
             to_later(d).start()
 
-    for q in range(ttiles):
-        span = slice(q * 128, (q + 1) * 128)
-        cc = wide(column(carry[q:q + 1, :]))
-        pc = column(past[q:q + 1, :])
-        u[span, :] = u[span, :] + cc * a
-        u[span, width - 128:] = u[span, width - 128:] + pc * edge[:, width - 128:]
-
-    loads[7].wait()
     for k in range(parts):
         rows = slice(k * part, (k + 1) * part)
-        strain[rows, :] = (
-            mm(mats[0], xh[rows, :]) + mm(mats[0], xl[rows, :]) + mm(mats[1], xh[rows, :])
-        )
-        hi, lo = split(u[rows, :])
-        vel[rows, :] = u[rows, :] - (mm(mats[2], hi) + mm(mats[2], lo) + mm(mats[3], hi))
+        u = mm(xh[rows, :], vh[...]) + mm(xl[rows, :], vh[...]) + mm(xh[rows, :], vl[...])
+        hi, lo = split(u)
+        vel[rows, :] = u - (mm(mats[2], hi) + mm(mats[2], lo) + mm(mats[3], hi))
+
+    def flat(tile_rows, k):
+        return jnp.concatenate([tile_rows[k * per + q:k * per + q + 1] for q in range(per)], axis=1)
+
+    def put(ref, slot, row, value, order):
+        hi = value.astype(BF16).astype(F32)
+        lo = value - hi
+        for n, which in enumerate(order):
+            ref[slot, row + n:row + n + 1, :] = hi if which == "h" else lo
+
+    st_rows[...] = jnp.zeros_like(st_rows)
+    for k in range(parts):
+        both = jnp.concatenate([flat(carry, k), flat(past, k)] + [jnp.zeros((6, part), F32)], axis=0)
+        hi = both.astype(BF16).astype(F32)
+        rows16 = jnp.concatenate([hi, both - hi], axis=0).astype(BF16)
+        r = mm_nt(rows16, mats[2]) + mm_nt(rows16, mats[3])
+        kept = both - (r[0:8] + r[8:16])
+        st_cols[2 * k] = cols[0]
+        st_cols[2 * k + 1] = cols[1]
+        for n, coef in ((0, a), (1, edge)):
+            put(st_cols, 2 * k + 1, 9 + 3 * n, kept[n:n + 1], "hlh")
+            put(st_rows, 2 * k + 1, 9 + 3 * n, coef, "hhl")
 
     for d in range(n_tm - 1):
         @pl.when(i > d)
@@ -313,7 +349,6 @@
         now_u = [p + r for p, r in zip(now_u, add_u)]
         power = step @ power
 
-    st_rows[...] = jnp.zeros_like(st_rows)
     for k in range(parts):
         for n, now in enumerate((now_x, now_u)):
             for r in range(3):
@@ -338,15 +373,20 @@
             to_later(d).wait_send()
 
 
-def finish(strain, vel, st_rows, cols, strain_hbm, vel_hbm, buf, out_sem):
+def finish(strain, vel, st_rows, st_cols, strain_hbm, vel_hbm, buf, out_sem):
     slab = strain.shape[0]
-    part = cols.shape[1]
+    part = st_cols.shape[2]
+    piece = buf.shape[1]
     stores = []
-    for k in range(slab // part):
-        rows = slice(k * part, (k + 1) * part)
-        for n, (src, out) in enumerate(((strain, strain_hbm), (vel, vel_hbm))):
-            slot = 2 * k + n
-            buf[slot] = src[rows, :] + mm(cols[n], st_rows[slot].astype(BF16))
+    for n, (src, out) in enumerate(((strain, strain_hbm), (vel, vel_hbm))):
+        for p in range(slab // piece):
+            k = p * piece // part
+            rows = slice(p * piece, (p + 1) * piece)
+            at = slice(p * piece - k * part, (p + 1) * piece - k * part)
+            slot = n * (slab // piece) + p
+            buf[slot] = src[rows, :] + mm_tn(
+                st_cols[2 * k + n, :, at].astype(BF16), st_rows[2 * k + n].astype(BF16)
+            )
             copy = pltpu.make_async_copy(buf.at[slot], out.at[rows, :], out_sem.at[slot])
             copy.start()
             stores.append(copy)
@@ -365,15 +405,16 @@
     any_spec = pl.BlockSpec(memory_space=pl.ANY)
     local = pl.BlockSpec(memory_space=pltpu.VMEM)
     out = jax.ShapeDtypeStruct((slab, width), F32)
-    strain, vel, st_rows = pl.pallas_call(
+    strain, vel, st_rows, st_cols = pl.pallas_call(
         functools.partial(kernel, n_chan, n_tm, reach, trans),
         out_shape=(
             pltpu.VMEM((slab, width), F32),
             pltpu.VMEM((slab, width), F32),
             pltpu.VMEM((2 * parts, 16, width), F32),
+            pltpu.VMEM((2 * parts, 16, part), F32),
         ),
-        in_specs=[hbm] * 8,
-        out_specs=(local, local, local),
+        in_specs=[hbm] * 9,
+        out_specs=(local,) * 4,
         scratch_shapes=[
             pltpu.VMEM((slab, width), F32),
             pltpu.VMEM((1, width), F32),
@@ -383,18 +424,19 @@
             pltpu.VMEM(mats.shape, BF16),
             pltpu.VMEM(ends.shape, BF16),
             pltpu.VMEM(e_tiles.shape, F32),
+            pltpu.VMEM(cols.shape, F32),
             pltpu.VMEM((slab, width), BF16),
             pltpu.VMEM((slab, width), BF16),
             pltpu.VMEM((width, width), BF16),
             pltpu.VMEM((width, width), BF16),
-            pltpu.VMEM((slab, width), F32),
+            pltpu.VMEM((parts, 16, width), F32),
             pltpu.VMEM((ttiles + 4, 128), F32),
             pltpu.VMEM((ttiles + 4, 128), F32),
             pltpu.VMEM((reach, ttiles + 4, 128), F32),
             pltpu.VMEM((ttiles + 4, 128), F32),
             pltpu.VMEM((8, width), F32),
             pltpu.VMEM((n_tm - 1, 8, width), F32),
-            pltpu.SemaphoreType.DMA((8,)),
+            pltpu.SemaphoreType.DMA((9,)),
             pltpu.SemaphoreType.DMA((reach,)),
             pltpu.SemaphoreType.DMA((reach,)),
             pltpu.SemaphoreType.DMA,
@@ -410,7 +452,7 @@
             pltpu.with_memory_space_constraint(a, pltpu.HBM)
             for a in (
                 strain_rate, gauge[None, :], valid[None, :], segment[None, :], stencil,
-                jnp.asarray(mats), jnp.asarray(ends), jnp.asarray(e_tiles),
+                jnp.asarray(mats), jnp.asarray(ends), jnp.asarray(e_tiles), jnp.asarray(cols),
             )
         ],
     )
@@ -420,11 +462,11 @@
         in_specs=[local] * 4,
         out_specs=(any_spec, any_spec),
         scratch_shapes=[
-            pltpu.VMEM((2 * parts, part, width), F32),
-            pltpu.SemaphoreType.DMA((2 * parts,)),
+            pltpu.VMEM((2 * ttiles, 128, width), F32),
+            pltpu.SemaphoreType.DMA((2 * ttiles,)),
         ],
         compiler_params=pltpu.CompilerParams(vmem_limit_bytes=16 * 1024 * 1024),
-    )(strain, vel, st_rows, jnp.asarray(cols))
+    )(strain, vel, st_rows, st_cols)
 
 
 def solution(mesh):

time: 11.9 us -> 12.2 us (1.025)
  Pallas kernels: 11.1 us -> 11.4 us
    pallas_call x1, Pallas kernels: 9.55 us -> 9.78 us  [on_device(): pl.pallas_call(functools.partial(kernel, n_chan, n_tm, reach, trans), out...]
where the time goes in v3:
time: 12.2 us; the launch traced here: 12 us
  Pallas kernels  11.4 us (93%)
  between operations  0.64 us (5%)
    pallas_call x1, Pallas kernels, on_device(): pl.pallas_call(functools.partial(kernel, n_chan, n_tm, reach, trans), out...  9.78 us
    pallas_call x1, Pallas kernels, on_device(): pl.pallas_call(finish, out_shape=(out, out), in_specs=[local] * 4, out_sp...  1.59 us

profile of v3, /device:TPU:0, one launch (start us, length us, event | category | flops | bytes accessed | tf_op | source)
XLA Modules:
  0.0 12.0 jit_solution(13063510150022940550)
XLA Ops:
  0.6 9.8 %shard_map.104 = (f32[512,512]{1,0:T(8,128)S(1)}, f32[512,512]{1,0:T(8,128)S(1)}, f32[4,16,512]{2,1,0:T(8,128)S(1)}, f32[4,16,256]{2,1,0:T(8,128)S(1)}) custom-call(f32[512,512]{1,0:T(8,128)} %x_hbm.1, f32[1,512]{1,0:T(1,128)} %bitcast.3, s32[1,512]{1,0:T(1,128)} %bitcast.4, s32[1,512]{1,0:T(1,128)} %bitcast.5, f32[3,512]{1,0:T(4,128)} %sten_hbm.1, ...), custom_call_target="tpu_custom_call" | custom-call | tf_op jit(solution)/shard_map/pallas_call | solution.py:408
  10.4 1.6 %shard_map.105 = (f32[512,512]{1,0:T(8,128)}, f32[512,512]{1,0:T(8,128)}) custom-call(f32[512,512]{1,0:T(8,128)S(1)} %get-tuple-element.6.strain, f32[512,512]{1,0:T(8,128)S(1)} %get-tuple-element.7.vel, f32[4,16,512]{2,1,0:T(8,128)S(1)} %get-tuple-element.8.st_rows, f32[4,16,256]{2,1,0:T(8,128)S(1)} %get-tuple-element.9.st_cols), custom_call_target="tpu_custom_call" | custom-call | tf_op jit(solution)/shard_map/pallas_call | solution.py:459

commit v4 on v3

--- a/solution.py
+++ b/solution.py
@@ -178,48 +178,44 @@
     right_out[ttiles:, :] = jnp.broadcast_to(tail, (4, 128))
     left_out[ttiles:, :] = jnp.broadcast_to(head, (4, 128))
 
+    targets = (
+        jnp.minimum(reach, n_chan - 1 - j) + jnp.minimum(j, 1) + jnp.minimum(n_tm - 1, n_tm - 1 - i)
+    )
+    pl.semaphore_wait(barrier, targets)
+
+    def to_right(d):
+        return pltpu.make_async_remote_copy(
+            right_out, right_in.at[d], right_send.at[d], right_recv.at[d],
+            device_id={"chan": j + 1 + d, "tm": i},
+        )
+
+    def to_left():
+        return pltpu.make_async_remote_copy(
+            left_out, left_in, left_send, left_recv, device_id={"chan": j - 1, "tm": i}
+        )
+
+    def to_later(d):
+        return pltpu.make_async_remote_copy(
+            state_out, state_in.at[d], st_send.at[d], st_recv.at[d],
+            device_id={"chan": j, "tm": i + 1 + d},
+        )
+
+    for d in range(reach):
+        @pl.when(j + 1 + d < n_chan)
+        def _():
+            to_right(d).start()
+    @pl.when(j > 0)
+    def _():
+        to_left().start()
+
     for k in range(parts):
         rows = slice(k * part, (k + 1) * part)
         hi, lo = split(x[rows, :])
         xh[rows, :] = hi
         xl[rows, :] = lo
-    loads[8].wait()
     for k in range(parts):
         rows = slice(k * part, (k + 1) * part)
-        strain[rows, :] = (
-            mm(mats[0], xh[rows, :]) + mm(mats[0], xl[rows, :]) + mm(mats[1], xh[rows, :])
-        )
-
-    targets = (
-        jnp.minimum(reach, n_chan - 1 - j) + jnp.minimum(j, 1) + jnp.minimum(n_tm - 1, n_tm - 1 - i)
-    )
-    pl.semaphore_wait(barrier, targets)
-
-    def to_right(d):
-        return pltpu.make_async_remote_copy(
-            right_out, right_in.at[d], right_send.at[d], right_recv.at[d],
-            device_id={"chan": j + 1 + d, "tm": i},
-        )
-
-    def to_left():
-        return pltpu.make_async_remote_copy(
-            left_out, left_in, left_send, left_recv, device_id={"chan": j - 1, "tm": i}
-        )
-
-    def to_later(d):
-        return pltpu.make_async_remote_copy(
-            state_out, state_in.at[d], st_send.at[d], st_recv.at[d],
-            device_id={"chan": j, "tm": i + 1 + d},
-        )
-
-    for d in range(reach):
-        @pl.when(j + 1 + d < n_chan)
-        def _():
-            to_right(d).start()
-    @pl.when(j > 0)
-    def _():
-        to_left().start()
-
+        vel[rows, :] = mm(xh[rows, :], vh[...]) + mm(xl[rows, :], vh[...]) + mm(xh[rows, :], vl[...])
     for c in loads[5:8]:
         c.wait()
     ends_x, ends_u = [], []
@@ -304,9 +300,16 @@
         def _():
             to_later(d).start()
 
+    loads[8].wait()
     for k in range(parts):
         rows = slice(k * part, (k + 1) * part)
-        u = mm(xh[rows, :], vh[...]) + mm(xl[rows, :], vh[...]) + mm(xh[rows, :], vl[...])
+        strain[rows, :] = (
+            mm(mats[0], xh[rows, :]) + mm(mats[0], xl[rows, :]) + mm(mats[1], xh[rows, :])
+        )
+
+    for k in range(parts):
+        rows = slice(k * part, (k + 1) * part)
+        u = vel[rows, :]
         hi, lo = split(u)
         vel[rows, :] = u - (mm(mats[2], hi) + mm(mats[2], lo) + mm(mats[3], hi))
 

time: 12.2 us -> 11.6 us (0.951)
  Pallas kernels: 11.4 us -> 10.8 us
    pallas_call x1, Pallas kernels: 9.78 us -> 9.19 us  [on_device(): pl.pallas_call(functools.partial(kernel, n_chan, n_tm, reach, trans), out...]
where the time goes in v4:
time: 11.6 us; the launch traced here: 11.4 us
  Pallas kernels  10.8 us (93%)
  between operations  0.64 us (6%)
    pallas_call x1, Pallas kernels, on_device(): pl.pallas_call(functools.partial(kernel, n_chan, n_tm, reach, trans), out...  9.19 us
    pallas_call x1, Pallas kernels, on_device(): pl.pallas_call(finish, out_shape=(out, out), in_specs=[local] * 4, out_sp...  1.6 us

profile of v4, /device:TPU:0, one launch (start us, length us, event | category | flops | bytes accessed | tf_op | source)
XLA Modules:
  0.0 11.4 jit_solution(12338426456581601000)
XLA Ops:
  0.6 9.2 %shard_map.104 = (f32[512,512]{1,0:T(8,128)S(1)}, f32[512,512]{1,0:T(8,128)S(1)}, f32[4,16,512]{2,1,0:T(8,128)S(1)}, f32[4,16,256]{2,1,0:T(8,128)S(1)}) custom-call(f32[512,512]{1,0:T(8,128)} %x_hbm.1, f32[1,512]{1,0:T(1,128)} %bitcast.3, s32[1,512]{1,0:T(1,128)} %bitcast.4, s32[1,512]{1,0:T(1,128)} %bitcast.5, f32[3,512]{1,0:T(4,128)} %sten_hbm.1, ...), custom_call_target="tpu_custom_call" | custom-call | tf_op jit(solution)/shard_map/pallas_call | solution.py:411
  9.8 1.6 %shard_map.105 = (f32[512,512]{1,0:T(8,128)}, f32[512,512]{1,0:T(8,128)}) custom-call(f32[512,512]{1,0:T(8,128)S(1)} %get-tuple-element.6.strain, f32[512,512]{1,0:T(8,128)S(1)} %get-tuple-element.7.vel, f32[4,16,512]{2,1,0:T(8,128)S(1)} %get-tuple-element.8.st_rows, f32[4,16,256]{2,1,0:T(8,128)S(1)} %get-tuple-element.9.st_cols), custom_call_target="tpu_custom_call" | custom-call | tf_op jit(solution)/shard_map/pallas_call | solution.py:462

commit v5 on v4

--- a/solution.py
+++ b/solution.py
@@ -93,26 +93,6 @@
     j = lax.axis_index("chan")
     i = lax.axis_index("tm")
 
-    blank = jnp.where(lax.broadcasted_iota(jnp.int32, (ttiles + 4, 128), 0) < ttiles, 0.0, -1.0)
-    for d in range(reach):
-        right_in[d] = blank
-    left_in[...] = blank
-    for d in range(n_tm - 1):
-        state_in[d] = jnp.zeros((8, width), F32)
-
-    barrier = pltpu.get_barrier_semaphore()
-    for d in range(reach):
-        @pl.when(j > d)
-        def _():
-            pl.semaphore_signal(barrier, inc=1, device_id={"chan": j - 1 - d, "tm": i})
-    @pl.when(j < n_chan - 1)
-    def _():
-        pl.semaphore_signal(barrier, inc=1, device_id={"chan": j + 1, "tm": i})
-    for d in range(n_tm - 1):
-        @pl.when(i > d)
-        def _():
-            pl.semaphore_signal(barrier, inc=1, device_id={"chan": j, "tm": i - 1 - d})
-
     loads = [
         pltpu.make_async_copy(src, dst, in_sem.at[n])
         for n, (src, dst) in enumerate(
@@ -121,8 +101,29 @@
              (mats_hbm, mats)]
         )
     ]
-    for c in loads[:8]:
-        c.start()
+    for n in (4, 2, 0, 1, 3, 5, 6, 7):
+        loads[n].start()
+
+    blank = jnp.where(lax.broadcasted_iota(jnp.int32, (ttiles + 4, 128), 0) < ttiles, 0.0, -1.0)
+    for d in range(reach):
+        right_in[d] = blank
+    left_in[...] = blank
+    for d in range(n_tm - 1):
+        state_in[d] = jnp.zeros((8, width), F32)
+
+    barrier = pltpu.get_barrier_semaphore()
+    for d in range(reach):
+        @pl.when(j > d)
+        def _():
+            pl.semaphore_signal(barrier, inc=1, device_id={"chan": j - 1 - d, "tm": i})
+    @pl.when(j < n_chan - 1)
+    def _():
+        pl.semaphore_signal(barrier, inc=1, device_id={"chan": j + 1, "tm": i})
+    for d in range(n_tm - 1):
+        @pl.when(i > d)
+        def _():
+            pl.semaphore_signal(barrier, inc=1, device_id={"chan": j, "tm": i - 1 - d})
+
     for c in loads[:4]:
         c.wait()
 

time: 11.6 us -> 11.6 us (level)
  no operation moved by 1% of the time
where the time goes in v5:
time: 11.6 us; the launch traced here: 11.4 us
  Pallas kernels  10.8 us (93%)
  between operations  0.64 us (6%)
    pallas_call x1, Pallas kernels, on_device(): pl.pallas_call(functools.partial(kernel, n_chan, n_tm, reach, trans), out...  9.19 us
    pallas_call x1, Pallas kernels, on_device(): pl.pallas_call(finish, out_shape=(out, out), in_specs=[local] * 4, out_sp...  1.59 us

profile of v5, /device:TPU:0, one launch (start us, length us, event | category | flops | bytes accessed | tf_op | source)
XLA Modules:
  0.0 11.4 jit_solution(11233225012198266844)
XLA Ops:
  0.6 9.2 %shard_map.104 = (f32[512,512]{1,0:T(8,128)S(1)}, f32[512,512]{1,0:T(8,128)S(1)}, f32[4,16,512]{2,1,0:T(8,128)S(1)}, f32[4,16,256]{2,1,0:T(8,128)S(1)}) custom-call(f32[512,512]{1,0:T(8,128)} %x_hbm.1, f32[1,512]{1,0:T(1,128)} %bitcast.3, s32[1,512]{1,0:T(1,128)} %bitcast.4, s32[1,512]{1,0:T(1,128)} %bitcast.5, f32[3,512]{1,0:T(4,128)} %sten_hbm.1, ...), custom_call_target="tpu_custom_call" | custom-call | tf_op jit(solution)/shard_map/pallas_call | solution.py:412
  9.8 1.6 %shard_map.105 = (f32[512,512]{1,0:T(8,128)}, f32[512,512]{1,0:T(8,128)}) custom-call(f32[512,512]{1,0:T(8,128)S(1)} %get-tuple-element.6.strain, f32[512,512]{1,0:T(8,128)S(1)} %get-tuple-element.7.vel, f32[4,16,512]{2,1,0:T(8,128)S(1)} %get-tuple-element.8.st_rows, f32[4,16,256]{2,1,0:T(8,128)S(1)} %get-tuple-element.9.st_cols), custom_call_target="tpu_custom_call" | custom-call | tf_op jit(solution)/shard_map/pallas_call | solution.py:463
